TPU v7x, 32 devices: a whole 2x2x4 slice. The times are simulated.
32 devices in a mesh: row: 4 (over x, core), col: 8 (over z, y).
Axes of the slice: x: 2, y: 2, z: 4, core: 2. Of those that a mesh axis runs over, the one named last changes fastest.
Arguments:
- inputs: bfloat16 [128, 8192], P('col', 'row'), may hold values from -6 to 6
- out_grad: bfloat16 [128, 8192], P('col', 'row'), may hold values from -0.8984375 to 0.8984375
- gate_pre: bfloat16 [128, 16384], P('row', 'col'), may hold values from -6 to 6
- up_pre: bfloat16 [128, 16384], P('row', 'col'), may hold values from -6 to 6
- gate_weight: bfloat16 [8192, 16384], P('row', 'col'), may hold values from -0.0625 to 0.0625
- up_weight: bfloat16 [8192, 16384], P('row', 'col'), may hold values from -0.0625 to 0.0625
- down_weight: bfloat16 [16384, 8192], P('col', 'row'), may hold values from -0.0625 to 0.0625
Outputs:
- input_grad: bfloat16 [128, 8192], P('col', 'row')
- gate_grad: bfloat16 [8192, 16384], P('row', 'col')
- up_grad: bfloat16 [8192, 16384], P('row', 'col')
- down_grad: bfloat16 [16384, 8192], P('col', 'row')
All inputs are finite; a program needn't handle non-finite values.
Results may differ from a plain program's by a relative error of at most 0.028.
Values may be sent and summed in bfloat16 or wider, within the bound.
A program may use at most 128 MiB of HBM per device.

v0:
```python
import jax
import jax.numpy as jnp
from jax import lax
from jax.sharding import PartitionSpec as P


def derivatives(gate_pre, up_pre, hidden_grad):
    gate_f32 = gate_pre.astype(jnp.float32)
    up_f32 = up_pre.astype(jnp.float32)
    sigmoid = 1.0 / (1.0 + jnp.exp(-gate_f32))
    activated = gate_f32 * sigmoid
    hidden = (activated * up_f32).astype(jnp.bfloat16)
    gate_delta = (hidden_grad * up_f32 * sigmoid * (1.0 + gate_f32 * (1.0 - sigmoid))).astype(
        jnp.bfloat16
    )
    up_delta = (hidden_grad * activated).astype(jnp.bfloat16)
    return (hidden, gate_delta, up_delta)


def per_device(inputs, out_grad, gate_pre, up_pre, gate_weight, up_weight, down_weight):
    by_cols = (((1,), (1,)), ((), ()))
    by_rows = (((0,), (0,)), ((), ()))
    all_inputs, all_grads = (
        lax.all_gather(inputs, "col", axis=0, tiled=True),
        lax.all_gather(out_grad, "col", axis=0, tiled=True),
    )
    gate_all, up_all = (
        lax.all_gather(gate_pre, "row", axis=0, tiled=True),
        lax.all_gather(up_pre, "row", axis=0, tiled=True),
    )
    hidden_total = lax.psum(
        lax.dot_general(all_grads, down_weight, by_cols, preferred_element_type=jnp.float32).astype(
            jnp.bfloat16
        ),
        "row",
    ).astype(jnp.float32)
    hidden, gate_delta, up_delta = derivatives(gate_all, up_all, hidden_total)
    down_grad = lax.dot_general(
        hidden, all_grads, by_rows, preferred_element_type=jnp.float32
    ).astype(jnp.bfloat16)
    gate_grad = lax.dot_general(
        all_inputs, gate_delta, by_rows, preferred_element_type=jnp.float32
    ).astype(jnp.bfloat16)
    up_grad = lax.dot_general(
        all_inputs, up_delta, by_rows, preferred_element_type=jnp.float32
    ).astype(jnp.bfloat16)
    gate_part_sum = lax.dot_general(
        gate_delta, gate_weight, by_cols, preferred_element_type=jnp.float32
    )
    input_grad = lax.psum_scatter(
        (
            gate_part_sum
            + lax.dot_general(up_delta, up_weight, by_cols, preferred_element_type=jnp.float32)
        ).astype(jnp.bfloat16),
        "col",
        scatter_dimension=0,
        tiled=True,
    )
    return (input_grad, gate_grad, up_grad, down_grad)


def solution(mesh):
    in_specs = (
        P("col", "row"),
        P("col", "row"),
        P("row", "col"),
        P("row", "col"),
        P("row", "col"),
        P("row", "col"),
        P("col", "row"),
    )
    out_specs = (P("col", "row"), P("row", "col"), P("row", "col"), P("col", "row"))
    return jax.shard_map(
        per_device, mesh=mesh, in_specs=in_specs, out_specs=out_specs, check_vma=False
    )
```

profile of v0, /device:TPU:0, one launch (start us, length us, event | category | flops | bytes accessed | tf_op | source)
XLA Modules:
  0.0 172.3 jit_solution(12948631233562550232)
XLA Ops:
  7.2 0.0 copy-start.1
  7.2 0.0 copy-start.2
  7.2 0.0 all-reduce.2.cloned.1.call-start
  7.2 33.3 %all_gather.12 = bf16[128,2048]{1,0:T(8,128)(2,1)S(1)} all-gather(bf16[16,2048]{1,0:T(8,128)(2,1)} %param.8), channel_id=1, replica_groups=mesh['row'=4,'col'=8] {'col'}, dimensions={0}, use_global_device_ids=true | all-gather | bytes 589824 | tf_op jit(solution)/shard_map/all_gather | solution.py:25
  40.6 7.1 %convolution_convert_fusion.1 = bf16[128,2048]{1,0:T(8,128)(2,1)} fusion(bf16[128,2048]{1,0:T(8,128)(2,1)S(1)} %all_gather.12, bf16[2048,2048]{1,0:T(8,128)(2,1)} %param.13), kind=kOutput, calls=%fused_computation.4 | convolution fusion | flops 1074003968 | bytes 9437184 | tf_op jit(solution)/shard_map/dot_general | solution.py:32
  47.6 0.0 all-reduce.2.cloned.1.call-update
  47.7 0.0 reduce-scatter.2.cloned.1.call-start
  47.7 0.0 copy-done.1
  47.7 7.2 %all_gather.14 = bf16[128,2048]{1,0:T(8,128)(2,1)S(1)} all-gather(bf16[32,2048]{1,0:T(8,128)(2,1)S(1)} %copy-done.1), channel_id=1, replica_groups=mesh['row'=4,'col'=8] {'row'}, dimensions={0}, use_global_device_ids=true | all-gather | bytes 655360 | tf_op jit(solution)/shard_map/all_gather | solution.py:28
  54.9 0.0 copy-done.2
  54.9 9.2 %all_gather.13 = bf16[128,2048]{1,0:T(8,128)(2,1)S(1)} all-gather(bf16[32,2048]{1,0:T(8,128)(2,1)S(1)} %copy-done.2), channel_id=1, replica_groups=mesh['row'=4,'col'=8] {'row'}, dimensions={0}, use_global_device_ids=true | all-gather | bytes 655360 | tf_op jit(solution)/shard_map/all_gather | solution.py:29
  64.1 5.8 %convolution_convert_fusion = bf16[2048,2048]{1,0:T(8,128)(2,1)} fusion(bf16[128,2048]{1,0:T(8,128)(2,1)S(1)} %all_gather.12, bf16[128,2048]{1,0:T(8,128)(2,1)S(1)} %all_gather.13, bf16[128,2048]{1,0:T(8,128)(2,1)S(1)} %all_gather.14), kind=kOutput, calls=%fused_computation.2 | convolution fusion | flops 1080033280 | bytes 9961472 | tf_op jit(solution)/shard_map/dot_general | solution.py:38
  69.9 13.4 %all-reduce.2.cloned.1.call-done = bf16[128,2048]{1,0:T(8,128)(2,1)} async-done(((bf16[128,2048]{1,0:T(8,128)(2,1)}), bf16[128,2048]{1,0:T(8,128)(2,1)}) %all-reduce.2.cloned.1.call-update) | async-done | bytes 524304 | tf_op jit(solution)/shard_map/psum | solution.py:31
  83.3 0.0 copy-start
  83.3 6.6 %fusion.15 = f32[128,2048]{1,0:T(8,128)S(1)} fusion(bf16[2048,2048]{1,0:T(8,128)(2,1)} %param.11, bf16[128,2048]{1,0:T(8,128)(2,1)S(1)} %all_gather.13, bf16[128,2048]{1,0:T(8,128)(2,1)} %all-reduce.2.cloned.1.call-done, bf16[128,2048]{1,0:T(8,128)(2,1)S(1)} %all_gather.14), kind=kOutput, calls=%fused_computation.22 | convolution fusion | flops 1077149696 | bytes 11010048 | tf_op jit(solution)/shard_map/dot_general | solution.py:47
  90.0 0.0 copy-done
  90.0 0.0 copy-start.3
  90.0 7.2 %fusion = bf16[128,2048]{1,0:T(8,128)(2,1)} fusion(f32[128,2048]{1,0:T(8,128)S(1)} %fusion.15, bf16[2048,2048]{1,0:T(8,128)(2,1)} %param.12, bf16[128,2048]{1,0:T(8,128)(2,1)S(1)} %copy-done, bf16[128,2048]{1,0:T(8,128)(2,1)S(1)} %all_gather.14), kind=kOutput, calls=%fused_computation.5 | convolution fusion | flops 1076363264 | bytes 11010048 | tf_op jit(solution)/shard_map/dot_general | solution.py:53
  97.2 0.0 reduce-scatter.2.cloned.1.call-update
  97.2 0.0 copy-done.3
  97.2 32.3 %all_gather.15 = bf16[128,2048]{1,0:T(8,128)(2,1)S(1)} all-gather(bf16[16,2048]{1,0:T(8,128)(2,1)S(1)} %copy-done.3), channel_id=1, replica_groups=mesh['row'=4,'col'=8] {'col'}, dimensions={0}, use_global_device_ids=true | all-gather | bytes 589824 | tf_op jit(solution)/shard_map/all_gather | solution.py:24
  129.5 5.8 %convert_bitcast_fusion.1 = bf16[2048,2048]{0,1:T(8,128)(2,1)} fusion(bf16[128,2048]{1,0:T(8,128)(2,1)S(1)} %all_gather.15, bf16[128,2048]{1,0:T(8,128)(2,1)S(1)} %all_gather.13, bf16[128,2048]{1,0:T(8,128)(2,1)S(1)} %copy-done, bf16[128,2048]{1,0:T(8,128)(2,1)S(1)} %all_gather.14), kind=kOutput, calls=%fused_computation.1 | convolution fusion | flops 1081344000 | bytes 10485760 | tf_op jit(solution)/shard_map/dot_general | solution.py:41
  135.3 12.2 %copy.11 = bf16[2048,2048]{1,0:T(8,128)(2,1)} copy(bf16[2048,2048]{0,1:T(8,128)(2,1)} %convert_bitcast_fusion.1) | data formatting | bytes 16777216
  147.6 5.6 %convert_bitcast_fusion = bf16[2048,2048]{0,1:T(8,128)(2,1)} fusion(bf16[128,2048]{1,0:T(8,128)(2,1)S(1)} %all_gather.15, bf16[128,2048]{1,0:T(8,128)(2,1)S(1)} %copy-done, bf16[128,2048]{1,0:T(8,128)(2,1)S(1)} %all_gather.14), kind=kOutput, calls=%fused_computation | convolution fusion | flops 1080033280 | bytes 9961472 | tf_op jit(solution)/shard_map/dot_general | solution.py:44
  153.2 12.2 %copy.12 = bf16[2048,2048]{1,0:T(8,128)(2,1)} copy(bf16[2048,2048]{0,1:T(8,128)(2,1)} %convert_bitcast_fusion) | data formatting | bytes 16777216
  165.4 0.0 reduce-scatter.2.cloned.1.call-done
Async XLA Ops:
  7.2 40.5 %copy-start.1 = (bf16[32,2048]{1,0:T(8,128)(2,1)S(1)}, bf16[32,2048]{1,0:T(8,128)(2,1)}, u32[]{:S(2)}) copy-start(bf16[32,2048]{1,0:T(8,128)(2,1)} %param.9) | copy-start | bytes 393220
  7.2 47.7 %copy-start.2 = (bf16[32,2048]{1,0:T(8,128)(2,1)S(1)}, bf16[32,2048]{1,0:T(8,128)(2,1)}, u32[]{:S(2)}) copy-start(bf16[32,2048]{1,0:T(8,128)(2,1)} %param.10) | copy-start | bytes 393220
  7.2 76.2 %all-reduce.2.cloned.1.call-start = ((), (), s32[]{:S(2)}) async-start(), calls=%async_computation.1 | async-start | bytes 1048576 | tf_op jit(solution)/shard_map/psum | solution.py:31
  47.7 117.8 %reduce-scatter.2.cloned.1.call-start = ((), (), s32[]{:S(2)}) async-start(), calls=%async_computation.2 | async-start | bytes 589824 | tf_op jit(solution)/shard_map/reduce_scatter | solution.py:50
  83.3 6.6 %copy-start = (bf16[128,2048]{1,0:T(8,128)(2,1)S(1)}, bf16[128,2048]{1,0:T(8,128)(2,1)}, u32[]{:S(2)}) copy-start(bf16[128,2048]{1,0:T(8,128)(2,1)} %all-reduce.2.cloned.1.call-done) | copy-start | bytes 1572868
  90.0 7.2 %copy-start.3 = (bf16[16,2048]{1,0:T(8,128)(2,1)S(1)}, bf16[16,2048]{1,0:T(8,128)(2,1)}, u32[]{:S(2)}) copy-start(bf16[16,2048]{1,0:T(8,128)(2,1)} %param.7) | copy-start | bytes 196612
Sparse Core Ops, SparseCore 0:
  47.8 35.5 all-reduce.1
  97.3 61.9 reduce-scatter.1
where the time goes:
time: 173 us; the launch traced here: 172 us
  blocking collectives  82 us (47%)
  matrix products  38.1 us (22%)
  local copies, waits for them, and re-layouts  24.5 us (14%)
  between operations  14.1 us (8%)
  waiting for transfers between devices  13.4 us (8%)
    all_gather x1, blocking collectives, per_device(): lax.all_gather(out_grad, 'col', axis=0, tiled=True)  33.3 us
    all_gather x1, blocking collectives, per_device(): lax.all_gather(inputs, 'col', axis=0, tiled=True)  32.3 us
    unnamed x10, local copies, waits for them, and re-layouts  24.5 us
    psum x1, waiting for transfers between devices, per_device(): lax.psum(lax.dot_general(all_grads, down_weight, by_cols, preferred_eleme...  13.4 us
    all_gather x1, blocking collectives, per_device(): lax.all_gather(up_pre, 'row', axis=0, tiled=True)  9.23 us
    dot_general x1, matrix products, per_device(): lax.dot_general(up_delta, up_weight, by_cols, preferred_element_type=jnp....  7.19 us
    all_gather x1, blocking collectives, per_device(): lax.all_gather(gate_pre, 'row', axis=0, tiled=True)  7.18 us
    dot_general x1, matrix products, per_device(): lax.dot_general(all_grads, down_weight, by_cols, preferred_element_type=j...  7.06 us
  transfers between devices with their start and end apart: 2, of which 1 were waited for; matrix products, arithmetic and copies ran while one was open for 24% of the time, Pallas kernels for 0%

commit v1 on v0

v1 whole, which is shorter than its diff:
```python
import functools

import jax
import jax.numpy as jnp
from jax import lax
from jax.experimental import pallas as pl
from jax.experimental.pallas import tpu as pltpu
from jax.sharding import PartitionSpec as P

BF16 = jnp.bfloat16
F32 = jnp.float32
MESH = pl.DeviceIdType.MESH
CHUNKS = 4
BY_COLS = (((1,), (1,)), ((), ()))
BY_ROWS = (((0,), (0,)), ((), ()))


class Ring:
    def __init__(self, name, size):
        self.name = name
        self.outers = size // 2
        self.index = lax.axis_index(name)
        self.pair = lax.rem(self.index, 2)
        self.outer = self.index // 2
        self.partner = self.outer * 2 + (1 - self.pair)

    def ahead(self, step):
        return lax.rem(self.outer + step, self.outers) * 2 + self.pair

    def behind_outer(self, step):
        return lax.rem(self.outer + self.outers - step, self.outers)

    def copy(self, src, dst, send_sem, recv_sem, target):
        return pltpu.make_async_remote_copy(
            src_ref=src,
            dst_ref=dst,
            send_sem=send_sem,
            recv_sem=recv_sem,
            device_id={self.name: target},
            device_id_type=MESH,
        )

    def everyone(self):
        return [self.partner] + [self.ahead(step) for step in range(1, self.outers)]


class Gather:
    def __init__(self, ring, held, send, recv):
        self.ring, self.held = ring, held
        n = ring.outers
        own = held.at[ring.index]
        self.direct = [
            ring.copy(own, own, send.at[s], recv.at[s], ring.ahead(s)) for s in range(1, n)
        ]
        self.relays = []
        for s in range(n):
            block = held.at[ring.behind_outer(s) * 2 + ring.pair]
            self.relays.append(
                ring.copy(block, block, send.at[n + s], recv.at[n + s], ring.partner)
            )

    def start(self):
        for copy in self.direct:
            copy.start()
        self.relays[0].start()

    def relay(self):
        for s in range(1, self.ring.outers):
            self.direct[s - 1].wait_recv()
            self.relays[s].start()

    def finish(self):
        for copy in self.relays:
            copy.wait_recv()

    def drain(self):
        for copy in self.direct + self.relays:
            copy.wait_send()


def main_kernel(
    n_row,
    n_col,
    inputs_ref,
    grads_ref,
    gate_ref,
    up_ref,
    gate_w_hbm,
    up_w_hbm,
    down_w_hbm,
    all_inputs_ref,
    all_grads_ref,
    hidden_ref,
    gate_delta_ref,
    up_delta_ref,
    input_grad_ref,
    held_grads,
    held_inputs,
    held_gate,
    held_up,
    gate_w,
    up_w,
    down_w,
    gate_factor,
    up_factor,
    pair_out,
    pair_in,
    own_half,
    outer_held,
    totals,
    part_out,
    part_in,
    part_own,
    sum_out,
    sum_in,
    load_sem,
    grads_send,
    grads_recv,
    inputs_send,
    inputs_recv,
    gate_send,
    gate_recv,
    up_send,
    up_recv,
    pair_send,
    pair_recv,
    outer_send,
    outer_recv,
    total_send,
    total_recv,
    part_send,
    part_recv,
    sum_send,
    sum_recv,
):
    row = Ring("row", n_row)
    col = Ring("col", n_col)
    rows_c, width = grads_ref.shape
    rows_r, hid = gate_ref.shape
    tokens = rows_c * n_col
    half = tokens // 2
    step_f = hid // CHUNKS
    step_d = width // CHUNKS
    outers_r, outers_c = row.outers, col.outers

    loads = []
    for j in range(CHUNKS):
        here = pl.ds(j * step_f, step_f)
        loads.append(pltpu.make_async_copy(down_w_hbm.at[here], down_w.at[here], load_sem.at[j]))
    for j in range(CHUNKS):
        here = pl.ds(j * step_d, step_d)
        loads.append(
            pltpu.make_async_copy(gate_w_hbm.at[here], gate_w.at[here], load_sem.at[CHUNKS + j])
        )
        loads.append(
            pltpu.make_async_copy(up_w_hbm.at[here], up_w.at[here], load_sem.at[2 * CHUNKS + j])
        )
    for load in loads:
        load.start()

    held_grads[col.index] = grads_ref[...]
    held_inputs[col.index] = inputs_ref[...]
    held_gate[row.index] = gate_ref[...]
    held_up[row.index] = up_ref[...]

    barrier = pltpu.get_barrier_semaphore()
    greeted = 0
    for ring in (row, col):
        for target in ring.everyone():
            pl.semaphore_signal(
                barrier, inc=1, device_id={ring.name: target}, device_id_type=MESH
            )
            greeted += 1
    pl.semaphore_wait(barrier, greeted)

    grads = Gather(col, held_grads, grads_send, grads_recv)
    gates = Gather(row, held_gate, gate_send, gate_recv)
    ups = Gather(row, held_up, up_send, up_recv)
    features = Gather(col, held_inputs, inputs_send, inputs_recv)
    grads.start()
    gates.start()
    ups.start()
    grads.relay()
    features.start()
    gates.relay()
    ups.relay()
    grads.finish()
    all_grads = held_grads[...].reshape(tokens, width)
    all_grads_ref[...] = all_grads

    def pair_copy(j):
        return row.copy(pair_out.at[j], pair_in.at[j], pair_send.at[j], pair_recv.at[j], row.partner)

    def outer_copy(j, s):
        own = outer_held.at[j, row.outer]
        return row.copy(own, own, outer_send.at[j, s], outer_recv.at[j, s], row.ahead(s))

    def total_copy(j):
        own = totals.at[j, row.pair]
        return row.copy(own, own, total_send.at[j], total_recv.at[j], row.partner)

    def hidden_part(j):
        loads[j].wait()
        part = lax.dot_general(
            held_grads[...].reshape(tokens, width),
            down_w[j * step_f : (j + 1) * step_f, :],
            BY_COLS,
            preferred_element_type=F32,
        )
        first, second = part[:half], part[half:]
        is_first = row.pair == 0
        pair_out[j] = jnp.where(is_first, second, first).astype(BF16)
        own_half[j] = jnp.where(is_first, first, second)
        pair_copy(j).start()

    def pair_sum(j):
        pair_copy(j).wait_recv()
        outer_held[j, row.outer] = (own_half[j] + pair_in[j].astype(F32)).astype(BF16)
        for s in range(1, outers_r):
            outer_copy(j, s).start()

    def outer_sum(j):
        for s in range(1, outers_r):
            outer_copy(j, s).wait_recv()
        total = outer_held[j, 0].astype(F32)
        for o in range(1, outers_r):
            total = total + outer_held[j, o].astype(F32)
        totals[j, row.pair] = total.astype(BF16)
        total_copy(j).start()

    def deltas(j):
        total_copy(j).wait_recv()
        here = slice(j * step_f, (j + 1) * step_f)
        total = totals[j].reshape(tokens, step_f).astype(F32)
        gate_delta_ref[:, here] = (total * gate_factor[:, here]).astype(BF16)
        up_delta_ref[:, here] = (total * up_factor[:, here]).astype(BF16)

    def activations():
        for r in range(n_row):
            here = slice(r * rows_r, (r + 1) * rows_r)
            gate_f32 = held_gate[r].astype(F32)
            up_f32 = held_up[r].astype(F32)
            sigmoid = 1.0 / (1.0 + jnp.exp(-gate_f32))
            activated = gate_f32 * sigmoid
            hidden_ref[here, :] = (activated * up_f32).astype(BF16)
            gate_factor[here, :] = up_f32 * sigmoid * (1.0 + gate_f32 * (1.0 - sigmoid))
            up_factor[here, :] = activated

    for j in range(CHUNKS):
        hidden_part(j)
        if j >= 1:
            pair_sum(j - 1)
    pair_sum(CHUNKS - 1)
    gates.finish()
    ups.finish()
    activations()
    features.relay()
    for j in range(CHUNKS):
        outer_sum(j)
        if j >= 1:
            deltas(j - 1)
    deltas(CHUNKS - 1)

    def part_copy(j):
        return col.copy(part_out.at[j], part_in.at[j], part_send.at[j], part_recv.at[j], col.partner)

    def sum_copy(j, s):
        target = col.ahead(s)
        return col.copy(
            sum_out.at[j, target // 2],
            sum_in.at[j, s],
            sum_send.at[j, s],
            sum_recv.at[j, s],
            target,
        )

    def input_part(j):
        loads[CHUNKS + 2 * j].wait()
        loads[CHUNKS + 2 * j + 1].wait()
        here = slice(j * step_d, (j + 1) * step_d)
        part = lax.dot_general(
            gate_delta_ref[...], gate_w[here, :], BY_COLS, preferred_element_type=F32
        ) + lax.dot_general(up_delta_ref[...], up_w[here, :], BY_COLS, preferred_element_type=F32)
        part = part.reshape(outers_c, 2, rows_c, step_d)
        even, odd = part[:, 0], part[:, 1]
        is_even = col.pair == 0
        part_out[j] = jnp.where(is_even, odd, even).astype(BF16)
        part_own[j] = jnp.where(is_even, even, odd)
        part_copy(j).start()

    def part_sum(j):
        part_copy(j).wait_recv()
        total = part_own[j] + part_in[j].astype(F32)
        part_own[j] = total
        sum_out[j] = total.astype(BF16)
        for s in range(1, outers_c):
            sum_copy(j, s).start()

    for j in range(CHUNKS):
        input_part(j)
        if j >= 1:
            part_sum(j - 1)
    part_sum(CHUNKS - 1)
    features.finish()
    all_inputs_ref[...] = held_inputs[...].reshape(tokens, width)
    for j in range(CHUNKS):
        total = part_own[j, col.outer]
        for s in range(1, outers_c):
            sum_copy(j, s).wait_recv()
            total = total + sum_in[j, s].astype(F32)
        input_grad_ref[:, j * step_d : (j + 1) * step_d] = total.astype(BF16)

    for gather in (grads, gates, ups, features):
        gather.drain()
    for j in range(CHUNKS):
        pair_copy(j).wait_send()
        total_copy(j).wait_send()
        part_copy(j).wait_send()
        for s in range(1, outers_r):
            outer_copy(j, s).wait_send()
        for s in range(1, outers_c):
            sum_copy(j, s).wait_send()


def main_call(n_row, n_col, inputs, out_grad, gate_pre, up_pre, gate_weight, up_weight, down_weight):
    rows_c, width = inputs.shape
    rows_r, hid = gate_pre.shape
    tokens = rows_c * n_col
    half = tokens // 2
    step_f, step_d = hid // CHUNKS, width // CHUNKS
    outers_r, outers_c = n_row // 2, n_col // 2
    vmem = pl.BlockSpec(memory_space=pltpu.VMEM)
    anywhere = pl.BlockSpec(memory_space=pl.ANY)
    dma = pltpu.SemaphoreType.DMA
    wide = jax.ShapeDtypeStruct((tokens, width), BF16)
    deep = jax.ShapeDtypeStruct((tokens, hid), BF16)
    gather_sems = [dma((n_col,))] * 4 + [dma((n_row,))] * 4
    return pl.pallas_call(
        functools.partial(main_kernel, n_row, n_col),
        out_shape=(wide, wide, deep, deep, deep, jax.ShapeDtypeStruct((rows_c, width), BF16)),
        in_specs=[vmem] * 4 + [anywhere] * 3,
        out_specs=[vmem] * 6,
        scratch_shapes=[
            pltpu.VMEM((n_col, rows_c, width), BF16),
            pltpu.VMEM((n_col, rows_c, width), BF16),
            pltpu.VMEM((n_row, rows_r, hid), BF16),
            pltpu.VMEM((n_row, rows_r, hid), BF16),
            pltpu.VMEM((width, hid), BF16),
            pltpu.VMEM((width, hid), BF16),
            pltpu.VMEM((hid, width), BF16),
            pltpu.VMEM((tokens, hid), F32),
            pltpu.VMEM((tokens, hid), F32),
            pltpu.VMEM((CHUNKS, half, step_f), BF16),
            pltpu.VMEM((CHUNKS, half, step_f), BF16),
            pltpu.VMEM((CHUNKS, half, step_f), F32),
            pltpu.VMEM((CHUNKS, outers_r, half, step_f), BF16),
            pltpu.VMEM((CHUNKS, 2, half, step_f), BF16),
            pltpu.VMEM((CHUNKS, outers_c, rows_c, step_d), BF16),
            pltpu.VMEM((CHUNKS, outers_c, rows_c, step_d), BF16),
            pltpu.VMEM((CHUNKS, outers_c, rows_c, step_d), F32),
            pltpu.VMEM((CHUNKS, outers_c, rows_c, step_d), BF16),
            pltpu.VMEM((CHUNKS, outers_c, rows_c, step_d), BF16),
            dma((3 * CHUNKS,)),
        ]
        + gather_sems
        + [dma((CHUNKS,)), dma((CHUNKS,))]
        + [dma((CHUNKS, outers_r)), dma((CHUNKS, outers_r))]
        + [dma((CHUNKS,)), dma((CHUNKS,))]
        + [dma((CHUNKS,)), dma((CHUNKS,))]
        + [dma((CHUNKS, outers_c)), dma((CHUNKS, outers_c))],
        compiler_params=pltpu.CompilerParams(
            collective_id=0, has_side_effects=True, vmem_limit_bytes=58 * 1024 * 1024
        ),
        cost_estimate=pl.CostEstimate(
            flops=6 * tokens * width * hid,
            bytes_accessed=6 * width * hid,
            transcendentals=tokens * hid,
        ),
        name="main",
    )(inputs, out_grad, gate_pre, up_pre, gate_weight, up_weight, down_weight)


def grads_kernel(
    inputs_ref, hidden_ref, gate_delta, up_delta, grads, gate_grad_ref, up_grad_ref, down_grad_ref
):
    def product(left, right):
        return lax.dot_general(left, right, BY_ROWS, preferred_element_type=F32).astype(BF16)

    left = inputs_ref[...]
    gate_grad_ref[...] = product(left, gate_delta[...])
    up_grad_ref[...] = product(left, up_delta[...])
    down_grad_ref[...] = product(hidden_ref[...], grads[...])


def grads_call(all_inputs, all_grads, hidden, gate_delta, up_delta):
    tokens, width = all_inputs.shape
    hid = hidden.shape[1]
    steps = min(8, width // 128, hid // 128)
    whole = pl.BlockSpec(memory_space=pltpu.VMEM)
    return pl.pallas_call(
        grads_kernel,
        grid=(steps,),
        out_shape=(
            jax.ShapeDtypeStruct((width, hid), BF16),
            jax.ShapeDtypeStruct((width, hid), BF16),
            jax.ShapeDtypeStruct((hid, width), BF16),
        ),
        in_specs=[
            pl.BlockSpec((tokens, width // steps), lambda i: (0, i)),
            pl.BlockSpec((tokens, hid // steps), lambda i: (0, i)),
            whole,
            whole,
            whole,
        ],
        out_specs=[
            pl.BlockSpec((width // steps, hid), lambda i: (i, 0)),
            pl.BlockSpec((width // steps, hid), lambda i: (i, 0)),
            pl.BlockSpec((hid // steps, width), lambda i: (i, 0)),
        ],
        compiler_params=pltpu.CompilerParams(vmem_limit_bytes=48 * 1024 * 1024),
        cost_estimate=pl.CostEstimate(
            flops=6 * tokens * width * hid,
            bytes_accessed=6 * width * hid,
            transcendentals=0,
        ),
        name="weight_grads",
    )(all_inputs, hidden, gate_delta, up_delta, all_grads)


def solution(mesh):
    n_row, n_col = mesh.shape["row"], mesh.shape["col"]

    def per_device(inputs, out_grad, gate_pre, up_pre, gate_weight, up_weight, down_weight):
        all_inputs, all_grads, hidden, gate_delta, up_delta, input_grad = main_call(
            n_row, n_col, inputs, out_grad, gate_pre, up_pre, gate_weight, up_weight, down_weight
        )
        gate_grad, up_grad, down_grad = grads_call(
            all_inputs, all_grads, hidden, gate_delta, up_delta
        )
        return (input_grad, gate_grad, up_grad, down_grad)

    in_specs = (
        P("col", "row"),
        P("col", "row"),
        P("row", "col"),
        P("row", "col"),
        P("row", "col"),
        P("row", "col"),
        P("col", "row"),
    )
    out_specs = (P("col", "row"), P("row", "col"), P("row", "col"), P("col", "row"))
    return jax.shard_map(
        per_device, mesh=mesh, in_specs=in_specs, out_specs=out_specs, check_vma=False
    )
```

time: 173 us -> 64.2 us (0.37)
  blocking collectives: 82 us -> 0 us
  Pallas kernels: 0 us -> 57.3 us
  matrix products: 38.1 us -> 0 us
  local copies, waits for them, and re-layouts: 24.5 us -> 5.83 us
  between operations: 14.1 us -> 0.66 us
  waiting for transfers between devices: 13.4 us -> 0 us
    all_gather x4 -> x0, blocking collectives: 82 us -> none  [the longest x1 33.3 us: per_device(): lax.all_gather(out_grad, 'col', axis=0, tiled=True)]
    pallas_call x0 -> x2, Pallas kernels: none -> 57.3 us  [the longest x1 46.8 us: main_call(): pl.pallas_call(functools.partial(main_kernel, n_row, n_col), out_shape=(w...]
    dot_general x6 -> x0, matrix products: 38.1 us -> none  [the longest x1 7.19 us: per_device(): lax.dot_general(up_delta, up_weight, by_cols, preferred_element_type=jnp....]
    unnamed x10 -> x13, local copies, waits for them, and re-layouts: 24.5 us -> 5.83 us
    psum x1 -> x0, waiting for transfers between devices: 13.4 us -> none  [per_device(): lax.psum(lax.dot_general(all_grads, down_weight, by_cols, preferred_eleme...]
  transfers between devices with their start and end apart: 2 -> 0, of which waited for: 1 -> 0; matrix products, arithmetic and copies ran while one was open for 24% -> 0% of each run, Pallas kernels for 0% -> 0%
where the time goes in v1:
time: 64.2 us; the launch traced here: 63.8 us
  Pallas kernels  57.3 us (89%)
  local copies, waits for them, and re-layouts  5.83 us (9%)
  between operations  0.66 us (1%)
    pallas_call x1, Pallas kernels, main_call(): pl.pallas_call(functools.partial(main_kernel, n_row, n_col), out_shape=(w...  46.8 us
    pallas_call x1, Pallas kernels, grads_call(): pl.pallas_call(grads_kernel, grid=(steps,), out_shape=(jax.ShapeDtypeStru...  10.5 us
    unnamed x13, local copies, waits for them, and re-layouts  5.83 us

profile of v1, /device:TPU:0, one launch (start us, length us, event | category | flops | bytes accessed | tf_op | source)
XLA Modules:
  0.0 63.8 jit_solution(16142887315703046964)
XLA Ops:
  0.6 46.8 %main.1 = (bf16[128,2048]{1,0:T(8,128)(2,1)}, bf16[128,2048]{1,0:T(8,128)(2,1)}, bf16[128,2048]{1,0:T(8,128)(2,1)}, bf16[128,2048]{1,0:T(8,128)(2,1)}, bf16[128,...) custom-call(bf16[16,2048]{1,0:T(8,128)(2,1)} %inputs_ref.1, bf16[16,2048]{1,0:T(8,128)(2,1)} %grads_ref.1, ...), custom_call_target="tpu_custom_call" | custom-call | flops 3221225472 | bytes 25165824 | tf_op jit(solution)/shard_map/main/pallas_call | solution.py:338
  47.5 0.0 copy-start
  47.5 1.0 %copy-done = bf16[128,2048]{1,0:T(8,128)(2,1)S(1)} copy-done((bf16[128,2048]{1,0:T(8,128)(2,1)S(1)}, bf16[128,2048]{1,0:T(8,128)(2,1)}, u32[]{:S(2)}) %copy-start) | copy-done | bytes 524312
  48.5 0.0 copy-start.1
  48.5 1.0 %copy-done.1 = bf16[128,2048]{1,0:T(8,128)(2,1)S(1)} copy-done((bf16[128,2048]{1,0:T(8,128)(2,1)S(1)}, bf16[128,2048]{1,0:T(8,128)(2,1)}, u32[]{:S(2)}) %copy-start.1) | copy-done | bytes 524312
  49.5 0.0 copy-start.2
  49.6 1.0 %copy-done.2 = bf16[128,2048]{1,0:T(8,128)(2,1)S(1)} copy-done((bf16[128,2048]{1,0:T(8,128)(2,1)S(1)}, bf16[128,2048]{1,0:T(8,128)(2,1)}, u32[]{:S(2)}) %copy-start.2) | copy-done | bytes 524312
  50.6 0.0 copy-start.3
  50.6 1.0 %copy-done.3 = bf16[128,2048]{1,0:T(8,128)(2,1)S(1)} copy-done((bf16[128,2048]{1,0:T(8,128)(2,1)S(1)}, bf16[128,2048]{1,0:T(8,128)(2,1)}, u32[]{:S(2)}) %copy-start.3) | copy-done | bytes 524312
  51.6 0.0 copy-start.4
  51.6 1.0 %copy-done.4 = bf16[128,2048]{1,0:T(8,128)(2,1)S(1)} copy-done((bf16[128,2048]{1,0:T(8,128)(2,1)S(1)}, bf16[128,2048]{1,0:T(8,128)(2,1)}, u32[]{:S(2)}) %copy-start.4) | copy-done | bytes 524312
  52.7 0.0 copy-start.5
  52.7 10.5 %weight_grads.1 = (bf16[2048,2048]{1,0:T(8,128)(2,1)}, bf16[2048,2048]{1,0:T(8,128)(2,1)}, bf16[2048,2048]{1,0:T(8,128)(2,1)}) custom-call(bf16[128,2048]{1,0:T(8,128)(2,1)S(1)} %copy-done, bf16[128,2048]{1,0:T(8,128)(2,1)S(1)} %copy-done.2, bf16[128,2048]{1,0:T(8,128)(2,1)S(1)} %copy-done.3, bf16[128,2048]{1,0:T(8,128)(2,1)S(1)} %copy-done.4, ...), custom_call_target="tpu_custom_call" | custom-call | flops 3221225472 | bytes 25165824 | tf_op jit(solution)/shard_map/weight_grads/pallas_call | solution.py:400
  63.2 0.0 copy-done.5
  63.2 0.6 copy.12
Async XLA Ops:
  47.5 1.0 %copy-start = (bf16[128,2048]{1,0:T(8,128)(2,1)S(1)}, bf16[128,2048]{1,0:T(8,128)(2,1)}, u32[]{:S(2)}) copy-start(bf16[128,2048]{1,0:T(8,128)(2,1)} %get-tuple-element.14.inputs_ref) | copy-start | bytes 1572868
  48.5 1.0 %copy-start.1 = (bf16[128,2048]{1,0:T(8,128)(2,1)S(1)}, bf16[128,2048]{1,0:T(8,128)(2,1)}, u32[]{:S(2)}) copy-start(bf16[128,2048]{1,0:T(8,128)(2,1)} %get-tuple-element.18.grads) | copy-start | bytes 1572868
  49.5 1.0 %copy-start.2 = (bf16[128,2048]{1,0:T(8,128)(2,1)S(1)}, bf16[128,2048]{1,0:T(8,128)(2,1)}, u32[]{:S(2)}) copy-start(bf16[128,2048]{1,0:T(8,128)(2,1)} %get-tuple-element.15.hidden_ref) | copy-start | bytes 1572868
  50.6 1.0 %copy-start.3 = (bf16[128,2048]{1,0:T(8,128)(2,1)S(1)}, bf16[128,2048]{1,0:T(8,128)(2,1)}, u32[]{:S(2)}) copy-start(bf16[128,2048]{1,0:T(8,128)(2,1)} %get-tuple-element.16.gate_delta) | copy-start | bytes 1572868
  51.6 1.0 %copy-start.4 = (bf16[128,2048]{1,0:T(8,128)(2,1)S(1)}, bf16[128,2048]{1,0:T(8,128)(2,1)}, u32[]{:S(2)}) copy-start(bf16[128,2048]{1,0:T(8,128)(2,1)} %get-tuple-element.17.up_delta) | copy-start | bytes 1572868
  52.7 10.5 %copy-start.5 = (bf16[16,2048]{1,0:T(8,128)(2,1)S(1)}, bf16[16,2048]{1,0:T(8,128)(2,1)}, u32[]{:S(2)}) copy-start(bf16[16,2048]{1,0:T(8,128)(2,1)} %get-tuple-element.26) | copy-start | bytes 196612

commit v2 on v1

--- a/solution.py
+++ b/solution.py
@@ -10,7 +10,7 @@
 BF16 = jnp.bfloat16
 F32 = jnp.float32
 MESH = pl.DeviceIdType.MESH
-CHUNKS = 4
+CHUNKS = 2
 BY_COLS = (((1,), (1,)), ((), ()))
 BY_ROWS = (((0,), (0,)), ((), ()))
 
@@ -173,6 +173,17 @@
             greeted += 1
     pl.semaphore_wait(barrier, greeted)
 
+    def activations():
+        for r in range(n_row):
+            here = slice(r * rows_r, (r + 1) * rows_r)
+            gate_f32 = held_gate[r].astype(F32)
+            up_f32 = held_up[r].astype(F32)
+            sigmoid = 1.0 / (1.0 + jnp.exp(-gate_f32))
+            activated = gate_f32 * sigmoid
+            hidden_ref[here, :] = (activated * up_f32).astype(BF16)
+            gate_factor[here, :] = up_f32 * sigmoid * (1.0 + gate_f32 * (1.0 - sigmoid))
+            up_factor[here, :] = activated
+
     grads = Gather(col, held_grads, grads_send, grads_recv)
     gates = Gather(row, held_gate, gate_send, gate_recv)
     ups = Gather(row, held_up, up_send, up_recv)
@@ -184,6 +195,9 @@
     features.start()
     gates.relay()
     ups.relay()
+    gates.finish()
+    ups.finish()
+    activations()
     grads.finish()
     all_grads = held_grads[...].reshape(tokens, width)
     all_grads_ref[...] = all_grads
@@ -235,25 +249,11 @@
         gate_delta_ref[:, here] = (total * gate_factor[:, here]).astype(BF16)
         up_delta_ref[:, here] = (total * up_factor[:, here]).astype(BF16)
 
-    def activations():
-        for r in range(n_row):
-            here = slice(r * rows_r, (r + 1) * rows_r)
-            gate_f32 = held_gate[r].astype(F32)
-            up_f32 = held_up[r].astype(F32)
-            sigmoid = 1.0 / (1.0 + jnp.exp(-gate_f32))
-            activated = gate_f32 * sigmoid
-            hidden_ref[here, :] = (activated * up_f32).astype(BF16)
-            gate_factor[here, :] = up_f32 * sigmoid * (1.0 + gate_f32 * (1.0 - sigmoid))
-            up_factor[here, :] = activated
-
     for j in range(CHUNKS):
         hidden_part(j)
         if j >= 1:
             pair_sum(j - 1)
     pair_sum(CHUNKS - 1)
-    gates.finish()
-    ups.finish()
-    activations()
     features.relay()
     for j in range(CHUNKS):
         outer_sum(j)
@@ -330,7 +330,7 @@
     step_f, step_d = hid // CHUNKS, width // CHUNKS
     outers_r, outers_c = n_row // 2, n_col // 2
     vmem = pl.BlockSpec(memory_space=pltpu.VMEM)
-    anywhere = pl.BlockSpec(memory_space=pl.ANY)
+    anywhere = pl.BlockSpec(memory_space=pltpu.HBM)
     dma = pltpu.SemaphoreType.DMA
     wide = jax.ShapeDtypeStruct((tokens, width), BF16)
     deep = jax.ShapeDtypeStruct((tokens, hid), BF16)
@@ -395,8 +395,9 @@
 def grads_call(all_inputs, all_grads, hidden, gate_delta, up_delta):
     tokens, width = all_inputs.shape
     hid = hidden.shape[1]
-    steps = min(8, width // 128, hid // 128)
-    whole = pl.BlockSpec(memory_space=pltpu.VMEM)
+    steps = min(4, width // 128, hid // 128)
+    deep = pl.BlockSpec((tokens, hid), lambda i: (0, 0))
+    wide = pl.BlockSpec((tokens, width), lambda i: (0, 0))
     return pl.pallas_call(
         grads_kernel,
         grid=(steps,),
@@ -408,16 +409,16 @@
         in_specs=[
             pl.BlockSpec((tokens, width // steps), lambda i: (0, i)),
             pl.BlockSpec((tokens, hid // steps), lambda i: (0, i)),
-            whole,
-            whole,
-            whole,
+            deep,
+            deep,
+            wide,
         ],
         out_specs=[
             pl.BlockSpec((width // steps, hid), lambda i: (i, 0)),
             pl.BlockSpec((width // steps, hid), lambda i: (i, 0)),
             pl.BlockSpec((hid // steps, width), lambda i: (i, 0)),
         ],
-        compiler_params=pltpu.CompilerParams(vmem_limit_bytes=48 * 1024 * 1024),
+        compiler_params=pltpu.CompilerParams(vmem_limit_bytes=58 * 1024 * 1024),
         cost_estimate=pl.CostEstimate(
             flops=6 * tokens * width * hid,
             bytes_accessed=6 * width * hid,

time: 64.2 us -> 57.6 us (0.90)
  local copies, waits for them, and re-layouts: 5.83 us -> 0.63 us
  Pallas kernels: 57.3 us -> 56.2 us
    unnamed x13 -> x3, local copies, waits for them, and re-layouts: 5.83 us -> 0.63 us
    pallas_call x1, Pallas kernels: 46.8 us -> 45.5 us  [main_call(): pl.pallas_call(functools.partial(main_kernel, n_row, n_col), out_shape=(w...]
where the time goes in v2:
time: 57.6 us; the launch traced here: 57.4 us
  Pallas kernels  56.2 us (98%)
  between operations  0.65 us (1%)
  local copies, waits for them, and re-layouts  0.63 us (1%)
    pallas_call x1, Pallas kernels, main_call(): pl.pallas_call(functools.partial(main_kernel, n_row, n_col), out_shape=(w...  45.5 us
    pallas_call x1, Pallas kernels, grads_call(): pl.pallas_call(grads_kernel, grid=(steps,), out_shape=(jax.ShapeDtypeStru...  10.6 us

profile of v2, /device:TPU:0, one launch (start us, length us, event | category | flops | bytes accessed | tf_op | source)
XLA Modules:
  0.0 57.4 jit_solution(17701486522713516077)
XLA Ops:
  0.6 45.5 %main.1 = (bf16[128,2048]{1,0:T(8,128)(2,1)}, bf16[128,2048]{1,0:T(8,128)(2,1)}, bf16[128,2048]{1,0:T(8,128)(2,1)}, bf16[128,2048]{1,0:T(8,128)(2,1)}, bf16[128,...) custom-call(bf16[16,2048]{1,0:T(8,128)(2,1)} %inputs_ref.1, bf16[16,2048]{1,0:T(8,128)(2,1)} %grads_ref.1, ...), custom_call_target="tpu_custom_call" | custom-call | flops 3221225472 | bytes 25165824 | tf_op jit(solution)/shard_map/main/pallas_call | solution.py:338
  46.2 0.0 copy-start
  46.2 10.6 %weight_grads.1 = (bf16[2048,2048]{1,0:T(8,128)(2,1)}, bf16[2048,2048]{1,0:T(8,128)(2,1)}, bf16[2048,2048]{1,0:T(8,128)(2,1)}) custom-call(bf16[128,2048]{1,0:T(8,128)(2,1)} %get-tuple-element.14.inputs_ref, bf16[128,2048]{1,0:T(8,128)(2,1)} %get-tuple-element.15.hidden_ref, bf16[128,2048]{1,0:T(8,128)(2,1)} %get-tuple-element.16.gate_delta, ...), custom_call_target="tpu_custom_call" | custom-call | flops 3221225472 | bytes 25165824 | tf_op jit(solution)/shard_map/weight_grads/pallas_call | solution.py:401
  56.8 0.0 copy-done
  56.8 0.6 %copy.12 = bf16[16,2048]{1,0:T(8,128)(2,1)} copy(bf16[16,2048]{1,0:T(8,128)(2,1)S(1)} %copy-done) | data formatting | bytes 131072
Async XLA Ops:
  46.2 10.6 %copy-start = (bf16[16,2048]{1,0:T(8,128)(2,1)S(1)}, bf16[16,2048]{1,0:T(8,128)(2,1)}, u32[]{:S(2)}) copy-start(bf16[16,2048]{1,0:T(8,128)(2,1)} %get-tuple-element.26) | copy-start | bytes 196612
